TPU v7x, 32 devices: a whole 2x2x4 slice. The times are simulated.
32 devices in a mesh: dp: 8 (over z, x), tensor: 4 (over y, core).
Axes of the slice: x: 2, y: 2, z: 4, core: 2. Of those that a mesh axis runs over, the one named last changes fastest.
Arguments:
- hidden: float32 [8192, 640], P('dp'), may hold values from -6 to 6
- seq_lengths: int32 [8, 4], P('dp'), may hold values from 0 to 1024, as said below
- input_scale: float32 [640], replicated, may hold values from 0.25 to 1.75
- w_query: float32 [640, 1024], P(None, 'tensor'), may hold values from -0.25 to 0.25
- w_key: float32 [640, 256], replicated, may hold values from -0.25 to 0.25
- w_value: float32 [640, 256], replicated, may hold values from -0.25 to 0.25
- query_scale: float32 [256], replicated, may hold values from 0.25 to 1.75
- key_scale: float32 [256], replicated, may hold values from 0.25 to 1.75
- w_out: float32 [1024, 640], P('tensor'), may hold values from -0.1875 to 0.1875
- post_attn_scale: float32 [640], replicated, may hold values from 0.25 to 1.75
- pre_ffn_scale: float32 [640], replicated, may hold values from 0.25 to 1.75
- w_gate: float32 [640, 2048], P(None, 'tensor'), may hold values from -0.25 to 0.25
- w_up: float32 [640, 2048], P(None, 'tensor'), may hold values from -0.25 to 0.25
- w_down: float32 [2048, 640], P('tensor'), may hold values from -0.125 to 0.125
- post_ffn_scale: float32 [640], replicated, may hold values from 0.25 to 1.75
- out_cotangent: float32 [8192, 640], P('dp'), may hold values from -6 to 6
Outputs:
- output: float32 [8192, 640], P('dp')
- hidden_grad: float32 [8192, 640], P('dp')
- input_scale_grad: float32 [640], replicated
- w_query_grad: float32 [640, 1024], P(None, 'tensor')
- w_key_grad: float32 [640, 256], replicated
- w_value_grad: float32 [640, 256], replicated
- query_scale_grad: float32 [256], replicated
- key_scale_grad: float32 [256], replicated
- w_out_grad: float32 [1024, 640], P('tensor')
- post_attn_scale_grad: float32 [640], replicated
- pre_ffn_scale_grad: float32 [640], replicated
- w_gate_grad: float32 [640, 2048], P(None, 'tensor')
- w_up_grad: float32 [640, 2048], P(None, 'tensor')
- w_down_grad: float32 [2048, 640], P('tensor')
- post_ffn_scale_grad: float32 [640], replicated
Inputs may be any that keep to these rules, and one draw needn't show every extreme that they name: `seq_lengths`: row d lists the lengths of the sequences held by index d of dp, in slot order, zeros for unused sequence slots; a row sums to at most 1024. In every draw exactly one row is a single sequence of 1024 tokens followed by zeros; every other row sums to between 128 and 896.
All inputs are finite; a program needn't handle non-finite values.
Results may differ from a plain program's by a relative error of at most 0.0003.
Values sent between devices are 32-bit elements; how exact they have to be, the bound alone decides.
A program may use at most 128 MiB of HBM per device.

v0:
```python
from functools import partial
import jax
import jax.numpy as jnp
from jax import lax
from jax.sharding import PartitionSpec as P

WINDOW = 512
epsilon = 1e-06
highest = lax.Precision.HIGHEST


def root_scale(values, gain):
    return values * lax.rsqrt(jnp.mean(values * values, axis=-1, keepdims=True) + epsilon) * gain


def rotate(values, cosine, sine):
    half_dim = values.shape[-1] // 2
    first_half = values[..., :half_dim]
    second_half = values[..., half_dim:]
    return jnp.concatenate(
        [first_half * cosine - second_half * sine, second_half * cosine + first_half * sine],
        axis=-1,
    )


def layout(lengths, row_count):
    bounds = jnp.concatenate([jnp.zeros((1,), jnp.int32), jnp.cumsum(lengths)])
    slot_index = jnp.arange(row_count, dtype=jnp.int32)
    segment = jnp.sum((slot_index[:, None] >= bounds[None, 1:]).astype(jnp.int32), axis=1)
    starts = jnp.max(jnp.where(bounds[None, :] <= slot_index[:, None], bounds[None, :], 0), axis=1)
    return (segment, slot_index - starts, slot_index < bounds[-1], slot_index)


def tables(positions, head_dim):
    half_dim = head_dim // 2
    frequency = 10000.0 ** (-2.0 * jnp.arange(half_dim).astype(jnp.float32) / head_dim)
    angles = positions.astype(jnp.float32)[:, None] * frequency[None, :]
    return (jnp.cos(angles), jnp.sin(angles))


def project_rows(inputs, gain, query_w, key_w, value_w, query_gain, key_gain, cosine, sine):
    normed = root_scale(inputs, gain)
    row_count = inputs.shape[0]
    queries = jnp.dot(normed, query_w, precision=highest).reshape(row_count, -1, key_w.shape[1])
    key_rows = jnp.dot(normed, key_w, precision=highest)
    value_rows = jnp.dot(normed, value_w, precision=highest)
    queries = rotate(root_scale(queries, query_gain), cosine[:, None, :], sine[:, None, :])
    key_rows = rotate(root_scale(key_rows, key_gain), cosine, sine)
    return (queries, key_rows, value_rows)


def middle(residual, branch, branch_gain, next_gain):
    hid_rows = residual + root_scale(branch, branch_gain)
    return (hid_rows, root_scale(hid_rows, next_gain))


def feed(inputs, gate_w, up_w, down_w):
    gated = jax.nn.gelu(jnp.dot(inputs, gate_w, precision=highest), approximate=True) * jnp.dot(
        inputs, up_w, precision=highest
    )
    return jnp.dot(gated, down_w, precision=highest)


def finish(branch, gain, residual):
    return residual + root_scale(branch, gain)


def on_device(
    hidden,
    seq_lengths,
    input_scale,
    w_query,
    w_key,
    w_value,
    query_scale,
    key_scale,
    w_out,
    post_attn_scale,
    pre_ffn_scale,
    w_gate,
    w_up,
    w_down,
    post_ffn_scale,
    out_cotangent,
):
    row_count = hidden.shape[0]
    head_dim = w_key.shape[1]
    head_count = w_query.shape[1] // head_dim
    scale = head_dim ** (-0.5)
    segment, positions, live_mask, slot_index = layout(seq_lengths[0], row_count)
    cosine, sine = tables(positions, head_dim)
    live_rows = live_mask.astype(jnp.float32)[:, None]
    (queries, key_rows, value_rows), project_back = jax.vjp(
        partial(project_rows, cosine=cosine, sine=sine),
        hidden,
        input_scale,
        w_query,
        w_key,
        w_value,
        query_scale,
        key_scale,
    )
    block_rows = min(512, row_count)
    block_count = row_count // block_rows
    key_pad = jnp.concatenate([jnp.zeros((block_rows, head_dim), jnp.float32), key_rows], axis=0)
    value_pad = jnp.concatenate(
        [jnp.zeros((block_rows, head_dim), jnp.float32), value_rows], axis=0
    )
    segment_pad = jnp.concatenate([jnp.full((block_rows,), -1, jnp.int32), segment])
    slot_pad = jnp.concatenate([jnp.arange(-block_rows, 0, dtype=jnp.int32), slot_index])

    def block_inputs(block_index):
        first_row = block_index * block_rows
        query_block = lax.dynamic_slice_in_dim(queries, first_row, block_rows, 0)
        key_block = lax.dynamic_slice_in_dim(key_pad, first_row, 2 * block_rows, 0)
        value_block = lax.dynamic_slice_in_dim(value_pad, first_row, 2 * block_rows, 0)
        distance = (
            lax.dynamic_slice_in_dim(slot_index, first_row, block_rows, 0)[:, None]
            - lax.dynamic_slice_in_dim(slot_pad, first_row, 2 * block_rows, 0)[None, :]
        )
        same_segment = (
            lax.dynamic_slice_in_dim(segment, first_row, block_rows, 0)[:, None]
            == lax.dynamic_slice_in_dim(segment_pad, first_row, 2 * block_rows, 0)[None, :]
        )
        allowed = same_segment & (distance >= 0) & (distance < WINDOW)
        scores = jnp.einsum("ihd,jd->hij", query_block, key_block, precision=highest) * scale
        scores = jnp.where(allowed[None], scores, -1e30)
        return (query_block, key_block, value_block, allowed, scores)

    def attend_block(block_index):
        query_block, key_block, value_block, allowed, scores = block_inputs(block_index)
        row_max = jnp.max(scores, axis=-1, keepdims=True)
        weights = jnp.exp(scores - row_max)
        weight_sum = jnp.sum(weights, axis=-1, keepdims=True)
        mixed_block = jnp.einsum(
            "hij,jd->ihd", weights / weight_sum, value_block, precision=highest
        )
        return (mixed_block, (row_max + jnp.log(weight_sum))[..., 0])

    def forward_block(block_index):
        return attend_block(block_index)

    mixed_blocks, log_sums = lax.map(forward_block, jnp.arange(block_count))
    mixed = mixed_blocks.reshape(row_count, head_count * head_dim)
    attn_part = jnp.dot(mixed, w_out, precision=highest)
    attn_whole = lax.psum(attn_part, "tensor")
    (hid_rows, ffn_in), middle_back = jax.vjp(
        middle, hidden, attn_whole, post_attn_scale, pre_ffn_scale
    )
    mlp_part, feed_back = jax.vjp(feed, ffn_in, w_gate, w_up, w_down)
    mlp_whole = lax.psum(mlp_part, "tensor")
    result, finish_back = jax.vjp(finish, mlp_whole, post_ffn_scale, hid_rows)
    output = result * live_rows
    out_grad = out_cotangent * live_rows
    mlp_grad, post_ffn_grad, hid_direct = finish_back(out_grad)
    ffn_in_part, gate_grad, up_grad, down_grad = feed_back(mlp_grad)
    ffn_in_grad = lax.psum(ffn_in_part, "tensor")
    hidden_direct, attn_grad, post_attn_grad, pre_ffn_grad = middle_back((hid_direct, ffn_in_grad))
    mixed_grad = jnp.dot(attn_grad, w_out.T, precision=highest).reshape(
        row_count, head_count, head_dim
    )
    out_weight_grad = jnp.dot(mixed.T, attn_grad, precision=highest)
    row_dots = jnp.sum(mixed_grad * mixed_blocks.reshape(row_count, head_count, head_dim), axis=-1)

    def attend_back(running, block_index):
        key_acc, value_acc = running
        query_block, key_block, value_block, allowed, scores = block_inputs(block_index)
        first_row = block_index * block_rows
        grad_block = lax.dynamic_slice_in_dim(mixed_grad, first_row, block_rows, 0)
        dots_block = lax.dynamic_slice_in_dim(row_dots, first_row, block_rows, 0)
        weights = jnp.where(allowed[None], jnp.exp(scores - log_sums[block_index][:, :, None]), 0.0)
        value_part = jnp.einsum("hij,ihd->jd", weights, grad_block, precision=highest)
        spread = jnp.einsum("ihd,jd->hij", grad_block, value_block, precision=highest)
        score_grad = weights * (spread - dots_block.T[:, :, None])
        query_part = jnp.einsum("hij,jd->ihd", score_grad, key_block, precision=highest) * scale
        key_part = jnp.einsum("hij,ihd->jd", score_grad, query_block, precision=highest) * scale
        key_acc = lax.dynamic_update_slice_in_dim(
            key_acc,
            lax.dynamic_slice_in_dim(key_acc, first_row, 2 * block_rows, 0) + key_part,
            first_row,
            0,
        )
        value_acc = lax.dynamic_update_slice_in_dim(
            value_acc,
            lax.dynamic_slice_in_dim(value_acc, first_row, 2 * block_rows, 0) + value_part,
            first_row,
            0,
        )
        return ((key_acc, value_acc), query_part)

    def back_block(running, block_index):
        return attend_back(running, block_index)

    empty_pad = jnp.zeros((row_count + block_rows, head_dim), jnp.float32)
    (key_acc, value_acc), query_parts = lax.scan(
        back_block, (empty_pad, empty_pad), jnp.arange(block_count)
    )
    query_grad = query_parts.reshape(row_count, head_count, head_dim)
    (
        hidden_part,
        input_part,
        query_w_grad,
        key_w_grad,
        value_w_grad,
        query_gain_grad,
        key_gain_grad,
    ) = project_back((query_grad, key_acc[block_rows:], value_acc[block_rows:]))
    hidden_attn, input_grad = lax.psum((hidden_part, input_part), "tensor")
    hidden_grad = hidden_direct + hidden_attn
    (
        query_w_grad,
        out_weight_grad,
        gate_grad,
        up_grad,
        down_grad,
        input_grad,
        post_attn_grad,
        pre_ffn_grad,
        post_ffn_grad,
    ) = lax.psum(
        (
            query_w_grad,
            out_weight_grad,
            gate_grad,
            up_grad,
            down_grad,
            input_grad,
            post_attn_grad,
            pre_ffn_grad,
            post_ffn_grad,
        ),
        "dp",
    )
    key_w_grad, value_w_grad, query_gain_grad, key_gain_grad = lax.psum(
        (key_w_grad, value_w_grad, query_gain_grad, key_gain_grad), ("dp", "tensor")
    )
    return (
        output,
        hidden_grad,
        input_grad,
        query_w_grad,
        key_w_grad,
        value_w_grad,
        query_gain_grad,
        key_gain_grad,
        out_weight_grad,
        post_attn_grad,
        pre_ffn_grad,
        gate_grad,
        up_grad,
        down_grad,
        post_ffn_grad,
    )


def solution(mesh):
    placed = (
        P("dp", None),
        P("dp", None),
        P(),
        P(None, "tensor"),
        P(),
        P(),
        P(),
        P(),
        P("tensor", None),
        P(),
        P(),
        P(None, "tensor"),
        P(None, "tensor"),
        P("tensor", None),
        P(),
        P("dp", None),
    )
    return jax.shard_map(
        on_device,
        mesh=mesh,
        in_specs=placed,
        out_specs=(
            P("dp", None),
            P("dp", None),
            P(),
            P(None, "tensor"),
            P(),
            P(),
            P(),
            P(),
            P("tensor", None),
            P(),
            P(),
            P(None, "tensor"),
            P(None, "tensor"),
            P("tensor", None),
            P(),
        ),
        check_vma=False,
    )
```

profile of v0, /device:TPU:0, one launch (start us, length us, event | category | flops | bytes accessed | tf_op | source)
XLA Modules:
  0.0 843.5 jit_solution(12557632794079602929)
XLA Ops:
  40.6 44.3 %while.26 = (s32[]{:T(128)}, f32[2,512,1,256]{1,0,3,2:T(2,128)}, f32[2,1,512]{2,1,0:T(1,128)}, s32[2]{0:T(128)S(1)}, f32[1536,256]{1,0:T(8,128)}, /*index=5*/s32...) while((s32[]{:T(128)}, f32[2,512,1,256]{1,0,3,2:T(2,128)}, ...), condition=%wide.region_9.10_spmd, body=%wide.region_6.9_spmd.sunk | while | flops 3228040704 | bytes 18932016 | solution.py:143
  52.4 10.3 %dynamic_update_slice.26 = f32[2,512,1,256]{1,0,3,2:T(2,128)} dynamic-update-slice(f32[2,512,1,256]{1,0,3,2:T(2,128)} %get-tuple-element.486, f32[1,512,1,256]{1,0,3,2:T(1,128)S(1)} %copy.111, s32[]{:T(128)S(6)} %copy.125, s32[]{:T(128)} %constant.60.clone.1..sunk, s32[]{:T(128)} %constant.60.clone.1..sunk, s32[]{:T(128)} %constant.60.clone.1..sunk) | dynamic-update-slice | bytes 1048580 | tf_op jit(solution)/shard_map/while/body/jit(dynamic_update_index_in_dim)/dynamic_update_slice | solution.py:143
  74.5 10.3 %dynamic_update_slice.26 = f32[2,512,1,256]{1,0,3,2:T(2,128)} dynamic-update-slice(f32[2,512,1,256]{1,0,3,2:T(2,128)} %get-tuple-element.486, f32[1,512,1,256]{1,0,3,2:T(1,128)S(1)} %copy.111, s32[]{:T(128)S(6)} %copy.125, s32[]{:T(128)} %constant.60.clone.1..sunk, s32[]{:T(128)} %constant.60.clone.1..sunk, s32[]{:T(128)} %constant.60.clone.1..sunk) | dynamic-update-slice | bytes 1048580 | tf_op jit(solution)/shard_map/while/body/jit(dynamic_update_index_in_dim)/dynamic_update_slice | solution.py:143
  91.9 62.3 %all-reduce.18.cloned.1.call-done = f32[1024,640]{1,0:T(8,128)} async-done(((f32[1024,640]{1,0:T(8,128)}), f32[1024,640]{1,0:T(8,128)}) %all-reduce.18.cloned.1.call-update) | async-done | bytes 2621456 | tf_op jit(solution)/shard_map/psum | solution.py:146
  171.0 7.4 fusion.121
  180.3 58.3 %all-reduce.20.cloned.1.call-done = f32[1024,640]{1,0:T(8,128)} async-done(((f32[1024,640]{1,0:T(8,128)}), f32[1024,640]{1,0:T(8,128)}) %all-reduce.20.cloned.1.call-update) | async-done | bytes 2621456 | tf_op jit(solution)/shard_map/psum | solution.py:151
  251.8 5.8 fusion.124
  257.7 8.5 %convolution_add_fusion = f32[1024,640]{1,0:T(8,128)} fusion(f32[1024,640]{1,0:T(8,128)S(1)} %fusion.124, f32[640,512]{1,0:T(8,128)S(1)} %copy-done.61, f32[1024,512]{1,0:T(8,128)S(1)} %copy-done.29, f32[1024,512]{1,0:T(8,128)S(1)} %fusion.133, f32[1024,512]{1,0:T(8,128)S(1)} %copy-done.44), kind=kOutput, calls=%fused_computation.94 | convolution fusion | flops 4037672960 | bytes 12845056 | tf_op jit(solution)/shard_map/transpose(jvp())/dot_general | solution.py:58
  266.3 9.4 %fusion.67 = f32[640,512]{1,0:T(8,128)} fusion(f32[1024,640]{1,0:T(8,128)} %copy-done.6, f32[640]{0:T(1024)S(1)} %copy-done.77, f32[1024]{0:T(1024)S(1)} %fusion.117, f32[1024,512]{1,0:T(8,128)} %copy-done.46, f32[1024,512]{1,0:T(8,128)} %copy-done.28), kind=kOutput, calls=%fused_computation.95 | convolution fusion | flops 4032561152 | bytes 8133120 | tf_op jit(solution)/shard_map/transpose(jvp())/dot_general | solution.py:58
  275.8 7.2 fusion.68
  283.0 43.4 %all-reduce.22.cloned.1.call-done = f32[1024,640]{1,0:T(8,128)} async-done(((f32[1024,640]{1,0:T(8,128)}), f32[1024,640]{1,0:T(8,128)}) %all-reduce.22.cloned.1.call-update) | async-done | bytes 2621456 | tf_op jit(solution)/shard_map/psum | solution.py:157
  342.3 68.0 %while.27 = (s32[]{:T(128)}, f32[1536,256]{0,1:T(8,128)}, f32[1536,256]{1,0:T(8,128)}, f32[2,512,1,256]{1,0,3,2:T(2,128)}, s32[2]{0:T(128)S(1)}, /*index=5*/s32[...) while((s32[]{:T(128)}, f32[1536,256]{0,1:T(8,128)}, ...), condition=%wide.region_21.22_spmd, body=%wide.region_20.21_spmd.sunk | while | flops 8060272640 | bytes 59294212 | solution.py:195
  366.0 10.3 %dynamic_update_slice.29 = f32[2,512,1,256]{1,0,3,2:T(2,128)} dynamic-update-slice(f32[2,512,1,256]{1,0,3,2:T(2,128)} %get-tuple-element.541, f32[1,512,1,256]{1,0,3,2:T(1,128)S(1)} %copy.116, s32[]{:T(128)S(6)} %copy.138, s32[]{:T(128)} %constant.60.clone.1..sunk.1, s32[]{:T(128)} %constant.60.clone.1..sunk.1, s32[]{:T(128)} %constant.60.clone.1..sunk.1) | dynamic-update-slice | bytes 1048580 | tf_op jit(solution)/shard_map/while/body/jit(dynamic_update_index_in_dim)/dynamic_update_slice | solution.py:143
  399.9 10.3 %dynamic_update_slice.29 = f32[2,512,1,256]{1,0,3,2:T(2,128)} dynamic-update-slice(f32[2,512,1,256]{1,0,3,2:T(2,128)} %get-tuple-element.541, f32[1,512,1,256]{1,0,3,2:T(1,128)S(1)} %copy.116, s32[]{:T(128)S(6)} %copy.138, s32[]{:T(128)} %constant.60.clone.1..sunk.1, s32[]{:T(128)} %constant.60.clone.1..sunk.1, s32[]{:T(128)} %constant.60.clone.1..sunk.1) | dynamic-update-slice | bytes 1048580 | tf_op jit(solution)/shard_map/while/body/jit(dynamic_update_index_in_dim)/dynamic_update_slice | solution.py:143
  430.7 6.1 multiply_reduce_fusion.3
  440.6 10.8 %fusion.119 = f32[512,640]{1,0:T(8,128)} fusion(f32[1024,512]{1,0:T(8,128)} %copy-done.43, f32[1024,512]{1,0:T(8,128)S(1)} %copy-done.31, f32[1024,640]{1,0:T(8,128)} %all-reduce.20.cloned.1.call-done, f32[1024,640]{1,0:T(8,128)} %param.35, f32[1024]{0:T(1024)S(1)} %copy-done.93, f32[1024]{0:T(1024)S(1)} %copy-done.76, f32[640]{0:T(1024)S(1)} %copy-done.91, ...), kind=kOutput, calls=%fused_computation.188 | convolution fusion | flops 4035182592 | bytes 10762752 | tf_op jit(solution)/shard_map/transpose(jvp())/dot_general | solution.py:61
  451.4 6.6 fusion.82
  458.1 5.6 fusion.129
  463.9 7.3 fusion.126
  475.3 39.7 %all-reduce.7 = (f32[256]{0:T(256)}, f32[256]{0:T(256)}) all-reduce(f32[256]{0:T(256)S(1)} %get-tuple-element.219, f32[256]{0:T(256)S(1)} %get-tuple-element.217), channel_id=1, replica_groups=mesh['dp'=8,'tensor'=4] {'dp','tensor'}, use_global_device_ids=true, to_apply=%region_33.34 | all-reduce | flops 512 | bytes 4096 | tf_op jit(solution)/shard_map/psum | solution.py:234
  515.0 7.1 psum.130
  522.0 36.2 %all-reduce.9 = (f32[640]{0:T(1024)}, f32[640]{0:T(1024)}, f32[640]{0:T(1024)}, f32[640]{0:T(1024)}) all-reduce(f32[640]{0:T(1024)S(1)} %psum.130, f32[640]{0:T(1024)S(1)} %get-tuple-element.213, f32[640]{0:T(1024)S(1)} %get-tuple-element.211, f32[640]{0:T(1024)S(1)} %copy-done.94), channel_id=1, replica_groups=mesh['dp'=8,'tensor'=4] {'dp'}, use_global_device_ids=true, to_apply=%region_28.29 | all-reduce | flops 2560 | bytes 20480 | tf_op jit(solution)/shard_map/psum | solution.py:220
  562.5 75.1 %all-reduce.26.cloned.1.call-done = (f32[640,256]{1,0:T(8,128)}, f32[640,256]{1,0:T(8,128)}) async-done(((f32[640,256]{1,0:T(8,128)}, f32[640,256]{1,0:T(8,128)}), (f32[640,256]{1,0:T(8,128)}, f32[640,256]{1,0:T(8,128)})) %all-reduce.26.cloned.1.call-update) | async-done | bytes 1310736 | tf_op jit(solution)/shard_map/psum | solution.py:234
  637.6 189.8 %all-reduce.28.cloned.1.call-done = (f32[640,256]{1,0:T(8,128)}, f32[256,640]{1,0:T(8,128)}, f32[640,512]{1,0:T(8,128)}, f32[640,512]{1,0:T(8,128)}, f32[512,640]{1,0:T(8,128)}) async-done(((f32[640,256]{1,0:T(8,128)}, f32[256,640]{1,0:T(8,128)}, f32[640,512]{1,0:T(8,128)}, f32[640,512]{1,0:T(8,128)}, f32[512,640]{1,0:T(8,128)}), (f32[640,256]{1,0:T(8,128)}, f32[256,640]{1,0:T(8,128)}, ...) | async-done | bytes 5242896 | tf_op jit(solution)/shard_map/psum | solution.py:220
  (359 shorter events, 193.2 us)
Async XLA Ops:
  7.2 163.9 %copy-start = (f32[512,640]{1,0:T(8,128)S(1)}, f32[512,640]{1,0:T(8,128)}, u32[]{:S(2)}) copy-start(f32[512,640]{1,0:T(8,128)} %param.33) | copy-start | bytes 3932164
  7.2 147.0 %all-reduce.18.cloned.1.call-start = ((), (), s32[]{:S(2)}) async-start(), calls=%async_computation | async-start | bytes 5242880 | tf_op jit(solution)/shard_map/psum | solution.py:146
  7.3 21.2 %copy-start.95 = (f32[128]{0:T(128)}, f32[128]{0:T(128)S(1)}, u32[]{:S(2)}) copy-start(f32[128]{0:T(128)S(1)} %multiply_power_fusion) | copy-start | bytes 1540
  9.1 19.4 %copy-start.67 = (f32[1024]{0:T(1024)}, f32[1024]{0:T(1024)S(1)}, u32[]{:S(2)}) copy-start(f32[1024]{0:T(1024)S(1)} %subtract_convert_fusion) | copy-start | bytes 12292
  91.5 64.9 %copy-start.73 = (f32[640]{0:T(1024)S(1)}, f32[640]{0:T(1024)}, u32[]{:S(2)}) copy-start(f32[640]{0:T(1024)} %param.29) | copy-start | bytes 7684
  91.5 147.1 %all-reduce.20.cloned.1.call-start = ((), (), s32[]{:S(2)}) async-start(), calls=%async_computation.1 | async-start | bytes 5242880 | tf_op jit(solution)/shard_map/psum | solution.py:151
  156.8 177.4 %copy-start.65 = (f32[1024]{0:T(1024)}, f32[1024]{0:T(1024)S(1)}, u32[]{:S(2)}) copy-start(f32[1024]{0:T(1024)S(1)} %fusion.116) | copy-start | bytes 12292
  178.4 62.3 %copy-start.90 = (f32[640]{0:T(1024)S(1)}, f32[640]{0:T(1024)}, u32[]{:S(2)}) copy-start(f32[640]{0:T(1024)} %param.34) | copy-start | bytes 7684
  178.4 148.0 %all-reduce.22.cloned.1.call-start = ((), (), s32[]{:S(2)}) async-start(), calls=%async_computation.2 | async-start | bytes 5242880 | tf_op jit(solution)/shard_map/psum | solution.py:157
  180.3 149.7 %copy-start.75 = (f32[1024]{0:T(1024)}, f32[1024]{0:T(1024)S(1)}, u32[]{:S(2)}) copy-start(f32[1024]{0:T(1024)S(1)} %fusion.112) | copy-start | bytes 12292
  266.3 292.0 %all-reduce.24.cloned.1.call-start = ((), (), s32[]{:S(2)}) async-start(), calls=%async_computation.3 | async-start | bytes 5242880 | tf_op jit(solution)/shard_map/psum | solution.py:208
  266.3 9.4 %copy-start.8 = (f32[1024,640]{1,0:T(8,128)S(1)}, f32[1024,640]{1,0:T(8,128)}, u32[]{:S(2)}) copy-start(f32[1024,640]{1,0:T(8,128)} %copy-done.6) | copy-start | bytes 7864324
  266.3 9.4 %copy-start.30 = (f32[1024,512]{1,0:T(8,128)S(1)}, f32[1024,512]{1,0:T(8,128)}, u32[]{:S(2)}) copy-start(f32[1024,512]{1,0:T(8,128)} %copy-done.28) | copy-start | bytes 6291460
  266.3 9.4 %copy-start.45 = (f32[1024,512]{1,0:T(8,128)S(1)}, f32[1024,512]{1,0:T(8,128)}, u32[]{:S(2)}) copy-start(f32[1024,512]{1,0:T(8,128)} %copy-done.43) | copy-start | bytes 6291460
  266.3 9.4 %copy-start.47 = (f32[1024,512]{1,0:T(8,128)S(1)}, f32[1024,512]{1,0:T(8,128)}, u32[]{:S(2)}) copy-start(f32[1024,512]{1,0:T(8,128)} %copy-done.46) | copy-start | bytes 6291460
  364.9 11.5 %copy-start.17 = (f32[1024,1,256]{2,1,0:T(1,128)S(1)}, f32[1024,1,256]{2,1,0:T(1,128)}, u32[]{:S(2)}) copy-start(f32[1024,1,256]{2,1,0:T(1,128)} %copy-done.16) | copy-start | bytes 3145732 | tf_op jit(solution)/shard_map/while
  398.8 11.5 %copy-start.17 = (f32[1024,1,256]{2,1,0:T(1,128)S(1)}, f32[1024,1,256]{2,1,0:T(1,128)}, u32[]{:S(2)}) copy-start(f32[1024,1,256]{2,1,0:T(1,128)} %copy-done.16) | copy-start | bytes 3145732 | tf_op jit(solution)/shard_map/while
  417.3 13.4 %copy-start.35 = (f32[1024,1,128]{0,2,1:T(8,128)}, f32[1024,1,128]{0,2,1:T(8,128)S(1)}, u32[]{:S(2)}) copy-start(f32[1024,1,128]{0,2,1:T(8,128)S(1)} %get-tuple-element.294) | copy-start | bytes 1572868
  417.3 13.4 %copy-start.37 = (f32[1024,1,128]{0,2,1:T(8,128)}, f32[1024,1,128]{0,2,1:T(8,128)S(1)}, u32[]{:S(2)}) copy-start(f32[1024,1,128]{0,2,1:T(8,128)S(1)} %get-tuple-element.295) | copy-start | bytes 1572868
  439.0 198.6 %all-reduce.26.cloned.1.call-start = ((), (), s32[]{:S(2)}) async-start(), calls=%async_computation.4 | async-start | bytes 2621440 | tf_op jit(solution)/shard_map/psum | solution.py:234
  440.6 10.8 %copy-start.5 = (f32[1024,640]{1,0:T(8,128)S(1)}, f32[1024,640]{1,0:T(8,128)}, u32[]{:S(2)}) copy-start(f32[1024,640]{1,0:T(8,128)} %param.20) | copy-start | bytes 7864324
  463.8 363.7 %all-reduce.28.cloned.1.call-start = ((), (), s32[]{:S(2)}) async-start(), calls=%async_computation.5 | async-start | bytes 10485760 | tf_op jit(solution)/shard_map/psum | solution.py:220
  475.2 46.8 %copy-start.94 = (f32[640]{0:T(1024)S(1)}, f32[640]{0:T(1024)}, u32[]{:S(2)}) copy-start(f32[640]{0:T(1024)} %get-tuple-element.209) | copy-start | bytes 7684
  637.6 193.9 %copy-start.62 = (f32[640,256]{1,0:T(8,128)S(1)}, f32[640,256]{1,0:T(8,128)}, u32[]{:S(2)}) copy-start(f32[640,256]{1,0:T(8,128)} %get-tuple-element.585) | copy-start | bytes 1966084
  (87 other events, 343.3 us)
Sparse Core Ops, SparseCore 0:
  91.6 62.5 all-reduce.17
  178.5 59.9 all-reduce.19
  266.4 59.9 all-reduce.21
  439.1 60.6 all-reduce.23
  505.9 131.7 all-reduce.25
  643.0 184.4 all-reduce.27
where the time goes:
time: 852 us; the launch traced here: 844 us
  waiting for transfers between devices  429 us (50%)
  matrix products  165 us (19%)
  local copies, waits for them, and re-layouts  100 us (12%)
  blocking collectives  82.9 us (10%)
  other arithmetic  43.3 us (5%)
  between operations  15.5 us (2%)
    psum x1, waiting for transfers between devices, on_device(): lax.psum((query_w_grad, out_weight_grad, gate_grad, up_grad, down_grad, i...  190 us
    psum x1, waiting for transfers between devices, on_device(): lax.psum((key_w_grad, value_w_grad, query_gain_grad, key_gain_grad), ('dp...  75.1 us
    psum x1, waiting for transfers between devices, on_device(): attn_whole = lax.psum(attn_part, 'tensor')  62.3 us
    psum x1, waiting for transfers between devices, on_device(): mlp_whole = lax.psum(mlp_part, 'tensor')  58.3 us
    dynamic_update_slice x10, local copies, waits for them, and re-layouts, on_device(): mixed_blocks, log_sums = lax.map(forward_block, jnp.arange(block_count))  44.6 us
    psum x1, waiting for transfers between devices, on_device(): ffn_in_grad = lax.psum(ffn_in_part, 'tensor')  43.4 us
    psum x1, blocking collectives, on_device(): lax.psum((key_w_grad, value_w_grad, query_gain_grad, key_gain_grad), ('dp...  39.7 us
    psum x1, blocking collectives, on_device(): lax.psum((query_w_grad, out_weight_grad, gate_grad, up_grad, down_grad, i...  36.2 us
  transfers between devices with their start and end apart: 6, of which 5 were waited for; matrix products, arithmetic and copies ran while one was open for 7% of the time, Pallas kernels for 0%

commit v1 on v0

--- a/solution.py
+++ b/solution.py
@@ -232,7 +232,7 @@
         "dp",
     )
     key_w_grad, value_w_grad, query_gain_grad, key_gain_grad = lax.psum(
-        (key_w_grad, value_w_grad, query_gain_grad, key_gain_grad), ("dp", "tensor")
+        lax.psum((key_w_grad, value_w_grad, query_gain_grad, key_gain_grad), "tensor"), "dp"
     )
     return (
         output,

time: 852 us -> 777 us (0.912)
  blocking collectives: 82.9 us -> 45.8 us
  local copies, waits for them, and re-layouts: 100 us -> 75.7 us
  waiting for transfers between devices: 429 us -> 407 us
  matrix products: 165 us -> 179 us
    psum x1 -> x0, waiting for transfers between devices: 75.1 us -> none  [on_device(): lax.psum((key_w_grad, value_w_grad, query_gain_grad, key_gain_grad), ('dp...]
    psum x1, waiting for transfers between devices: 0.01 us -> 54.5 us  [on_device(): hidden_attn, input_grad = lax.psum((hidden_part, input_part), 'tensor')]
    psum x1 -> x0, blocking collectives: 39.7 us -> none  [on_device(): lax.psum((key_w_grad, value_w_grad, query_gain_grad, key_gain_grad), ('dp...]
    dynamic_update_slice x10, local copies, waits for them, and re-layouts: 44.6 us -> 32.3 us  [on_device(): mixed_blocks, log_sums = lax.map(forward_block, jnp.arange(block_count))]
    psum x1, waiting for transfers between devices: 190 us -> 181 us  [on_device(): lax.psum((query_w_grad, out_weight_grad, gate_grad, up_grad, down_grad, i...]
    unnamed x195 -> x127, local copies, waits for them, and re-layouts: 18.7 us -> 15.7 us
  transfers between devices with their start and end apart: 6 -> 5, of which waited for: 5 -> 5; matrix products, arithmetic and copies ran while one was open for 7% -> 5% of each run, Pallas kernels for 0% -> 0%
where the time goes in v1:
time: 777 us; the launch traced here: 771 us
  waiting for transfers between devices  407 us (52%)
  matrix products  179 us (23%)
  local copies, waits for them, and re-layouts  75.7 us (10%)
  blocking collectives  45.8 us (6%)
  other arithmetic  40.9 us (5%)
  between operations  14.8 us (2%)
    psum x1, waiting for transfers between devices, on_device(): lax.psum((query_w_grad, out_weight_grad, gate_grad, up_grad, down_grad, i...  181 us
    psum x1, waiting for transfers between devices, on_device(): attn_whole = lax.psum(attn_part, 'tensor')  62.5 us
    psum x1, waiting for transfers between devices, on_device(): mlp_whole = lax.psum(mlp_part, 'tensor')  58.9 us
    psum x1, waiting for transfers between devices, on_device(): hidden_attn, input_grad = lax.psum((hidden_part, input_part), 'tensor')  54.5 us
    psum x1, waiting for transfers between devices, on_device(): ffn_in_grad = lax.psum(ffn_in_part, 'tensor')  49.4 us
    psum x1, blocking collectives, on_device(): lax.psum((query_w_grad, out_weight_grad, gate_grad, up_grad, down_grad, i...  39.9 us
    dynamic_update_slice x10, local copies, waits for them, and re-layouts, on_device(): mixed_blocks, log_sums = lax.map(forward_block, jnp.arange(block_count))  32.3 us
    dot_general x3, matrix products, feed(): return jnp.dot(gated, down_w, precision=highest)  23.9 us
  transfers between devices with their start and end apart: 5, of which 5 were waited for; matrix products, arithmetic and copies ran while one was open for 5% of the time, Pallas kernels for 0%

profile of v1, /device:TPU:0, one launch (start us, length us, event | category | flops | bytes accessed | tf_op | source)
XLA Modules:
  0.0 771.0 jit_solution(17321406752113947427)
XLA Ops:
  34.7 31.6 %while.26 = (s32[]{:T(128)}, f32[2,512,1,256]{1,0,3,2:T(2,128)S(1)}, f32[2,1,512]{2,1,0:T(1,128)S(1)}, s32[2]{0:T(128)S(1)}, f32[1536,256]{1,0:T(8,128)}, /*inde...) while((s32[]{:T(128)}, ...), condition=%wide.region_9.10_spmd, body=%wide.region_6.9_spmd.sunk | while | flops 3228040704 | bytes 12640524 | solution.py:143
  72.0 62.5 %all-reduce.17.cloned.1.call-done = f32[1024,640]{1,0:T(8,128)} async-done(((f32[1024,640]{1,0:T(8,128)}), f32[1024,640]{1,0:T(8,128)}) %all-reduce.17.cloned.1.call-update) | async-done | bytes 2621456 | tf_op jit(solution)/shard_map/psum | solution.py:146
  144.7 5.1 fusion.69
  151.2 7.6 fusion.121
  160.2 58.9 %all-reduce.19.cloned.1.call-done = f32[1024,640]{1,0:T(8,128)} async-done(((f32[1024,640]{1,0:T(8,128)}), f32[1024,640]{1,0:T(8,128)}) %all-reduce.19.cloned.1.call-update) | async-done | bytes 2621456 | tf_op jit(solution)/shard_map/psum | solution.py:151
  226.6 5.6 fusion.133
  232.3 5.8 fusion.124
  238.2 8.3 %convolution_add_fusion = f32[1024,640]{1,0:T(8,128)} fusion(f32[1024,640]{1,0:T(8,128)S(1)} %fusion.124, f32[640,512]{1,0:T(8,128)S(1)} %copy-done.54, f32[1024,512]{1,0:T(8,128)S(1)} %fusion.70, f32[1024,512]{1,0:T(8,128)S(1)} %fusion.133, f32[1024,512]{1,0:T(8,128)S(1)} %copy-done.37), kind=kOutput, calls=%fused_computation.94 | convolution fusion | flops 4037672960 | bytes 12845056 | tf_op jit(solution)/shard_map/transpose(jvp())/dot_general | solution.py:58
  246.5 10.7 %fusion.119 = f32[512,640]{1,0:T(8,128)} fusion(f32[1024,512]{1,0:T(8,128)} %copy-done.36, f32[1024,512]{1,0:T(8,128)S(1)} %fusion.70, f32[1024,640]{1,0:T(8,128)} %all-reduce.19.cloned.1.call-done, f32[1024,640]{1,0:T(8,128)} %param.35, f32[1024]{0:T(1024)S(1)} %multiply_multiply_fusion.15, f32[1024]{0:T(1024)S(1)} %fusion.112, f32[640]{0:T(1024)S(1)} %copy-done.62, ...), kind=kOutput, calls=%fused_computation.188 | convolution fusion | flops 4035182592 | bytes 10762752 | tf_op jit(solution)/shard_map/transpose(jvp())/dot_general | solution.py:61
  257.2 49.4 %all-reduce.21.cloned.1.call-done = f32[1024,640]{1,0:T(8,128)} async-done(((f32[1024,640]{1,0:T(8,128)}), f32[1024,640]{1,0:T(8,128)}) %all-reduce.21.cloned.1.call-update) | async-done | bytes 2621456 | tf_op jit(solution)/shard_map/psum | solution.py:157
  322.7 79.5 %while.27 = (s32[]{:T(128)}, f32[1536,256]{0,1:T(8,128)}, f32[1536,256]{1,0:T(8,128)}, f32[2,512,1,256]{1,0,3,2:T(2,128)}, s32[2]{0:T(128)S(1)}, /*index=5*/s32[...) while((s32[]{:T(128)}, f32[1536,256]{0,1:T(8,128)}, ...), condition=%wide.region_21.22_spmd, body=%wide.region_20.21_spmd.sunk | while | flops 8060272640 | bytes 63488508 | solution.py:195
  348.2 10.3 %dynamic_update_slice.29 = f32[2,512,1,256]{1,0,3,2:T(2,128)} dynamic-update-slice(f32[2,512,1,256]{1,0,3,2:T(2,128)} %get-tuple-element.547, f32[1,512,1,256]{1,0,3,2:T(1,128)S(1)} %copy.116, s32[]{:T(128)} %get-tuple-element.544, s32[]{:T(128)} %constant.60.clone.1..sunk.1, s32[]{:T(128)} %constant.60.clone.1..sunk.1, s32[]{:T(128)} %constant.60.clone.1..sunk.1) | dynamic-update-slice | bytes 1048580 | tf_op jit(solution)/shard_map/while/body/jit(dynamic_update_index_in_dim)/dynamic_update_slice | solution.py:143
  387.7 10.3 %dynamic_update_slice.29 = f32[2,512,1,256]{1,0,3,2:T(2,128)} dynamic-update-slice(f32[2,512,1,256]{1,0,3,2:T(2,128)} %get-tuple-element.547, f32[1,512,1,256]{1,0,3,2:T(1,128)S(1)} %copy.116, s32[]{:T(128)} %get-tuple-element.544, s32[]{:T(128)} %constant.60.clone.1..sunk.1, s32[]{:T(128)} %constant.60.clone.1..sunk.1, s32[]{:T(128)} %constant.60.clone.1..sunk.1) | dynamic-update-slice | bytes 1048580 | tf_op jit(solution)/shard_map/while/body/jit(dynamic_update_index_in_dim)/dynamic_update_slice | solution.py:143
  406.7 5.4 fusion.129
  412.1 6.7 fusion.130
  423.2 5.3 fusion.82
  432.0 7.7 multiply_reduce_fusion.3
  443.3 8.8 %fusion.67 = f32[640,512]{1,0:T(8,128)} fusion(f32[1024,640]{1,0:T(8,128)} %copy-done.9, f32[640]{0:T(1024)S(1)} %copy-done.59, f32[1024]{0:T(1024)S(1)} %fusion.117, f32[1024,512]{1,0:T(8,128)} %copy-done.39, f32[1024,512]{1,0:T(8,128)S(1)} %copy-done.28), kind=kOutput, calls=%fused_computation.95 | convolution fusion | flops 4032561152 | bytes 8133120 | tf_op jit(solution)/shard_map/transpose(jvp())/dot_general | solution.py:58
  452.2 7.2 fusion.68
  459.4 5.6 fusion.126
  469.1 54.5 %all-reduce.25.cloned.1.call-done = (f32[1024,640]{1,0:T(8,128)}, f32[640,256]{1,0:T(8,128)}, f32[640,256]{1,0:T(8,128)}) async-done(((f32[1024,640]{1,0:T(8,128)}, f32[640,256]{1,0:T(8,128)}, f32[640,256]{1,0:T(8,128)}), (f32[1024,640]{1,0:T(8,128)}, f32[640,256]{1,0:T(8,128)}, f32[640,256]{1,0:T(8,128)})) %all-reduce.25.cloned.1.call-update) | async-done | bytes 3932176 | tf_op jit(solution)/shard_map/psum | solution.py:208
  523.6 5.9 all-reduce.9
  529.5 39.9 %all-reduce.7 = (f32[640]{0:T(1024)}, f32[256]{0:T(256)}, f32[256]{0:T(256)}, f32[640]{0:T(1024)}, f32[640]{0:T(1024)}, /*index=5*/f32[640]{0:T(1024)}) all-reduce(f32[640]{0:T(1024)S(1)} %get-tuple-element.286, f32[256]{0:T(256)S(1)} %get-tuple-element.287, ...), channel_id=1, replica_groups=mesh['dp'=8,'tensor'=4] {'dp'}, use_global_device_ids=true, to_apply=%region_28.29 | all-reduce | flops 3072 | bytes 24576 | tf_op jit(solution)/shard_map/psum | solution.py:220
  574.0 181.3 %all-reduce.23.cloned.1.call-done = (f32[640,256]{1,0:T(8,128)}, f32[640,256]{1,0:T(8,128)}, f32[640,256]{1,0:T(8,128)}, f32[256,640]{1,0:T(8,128)}, f32[640,512...) async-done(((f32[640,256]{1,0:T(8,128)}, f32[640,256]{1,0:T(8,128)}, f32[640,256]{1,0:T(8,128)}, f32[256,640]{1,0:T(8,128)}, f32[640,512]{1,0:T(8,128)}, ...) | async-done | bytes 6553616 | tf_op jit(solution)/shard_map/psum | solution.py:220
  (283 shorter events, 185.7 us)
Async XLA Ops:
  7.2 144.0 %copy-start = (f32[512,640]{1,0:T(8,128)S(1)}, f32[512,640]{1,0:T(8,128)}, u32[]{:S(2)}) copy-start(f32[512,640]{1,0:T(8,128)} %param.33) | copy-start | bytes 3932164
  7.2 127.3 %all-reduce.17.cloned.1.call-start = ((), (), s32[]{:S(2)}) async-start(), calls=%async_computation | async-start | bytes 5242880 | tf_op jit(solution)/shard_map/psum | solution.py:146
  71.7 64.9 %copy-start.58 = (f32[640]{0:T(1024)S(1)}, f32[640]{0:T(1024)}, u32[]{:S(2)}) copy-start(f32[640]{0:T(1024)} %param.29) | copy-start | bytes 7684
  71.7 147.3 %all-reduce.19.cloned.1.call-start = ((), (), s32[]{:S(2)}) async-start(), calls=%async_computation.1 | async-start | bytes 5242880 | tf_op jit(solution)/shard_map/psum | solution.py:151
  144.7 101.8 %copy-start.27 = (f32[1024,512]{1,0:T(8,128)}, f32[1024,512]{1,0:T(8,128)S(1)}, u32[]{:S(2)}) copy-start(f32[1024,512]{1,0:T(8,128)S(1)} %fusion.70) | copy-start | bytes 6291460
  158.9 62.3 %copy-start.62 = (f32[640]{0:T(1024)S(1)}, f32[640]{0:T(1024)}, u32[]{:S(2)}) copy-start(f32[640]{0:T(1024)} %param.34) | copy-start | bytes 7684
  158.9 147.7 %all-reduce.21.cloned.1.call-start = ((), (), s32[]{:S(2)}) async-start(), calls=%async_computation.2 | async-start | bytes 5242880 | tf_op jit(solution)/shard_map/psum | solution.py:157
  246.5 277.1 %all-reduce.25.cloned.1.call-start = ((), (), s32[]{:S(2)}) async-start(), calls=%async_computation.4 | async-start | bytes 7864320 | tf_op jit(solution)/shard_map/psum | solution.py:208
  325.9 6.1 copy-start.15
  347.6 10.9 %copy-start.8 = (f32[1,512,1024]{1,2,0:T(8,128)S(1)}, f32[1,512,1024]{1,2,0:T(8,128)}, u32[]{:S(2)}) copy-start(f32[1,512,1024]{1,2,0:T(8,128)} %copy-done.7) | copy-start | bytes 6291460 | tf_op jit(solution)/shard_map/while
  365.5 6.1 copy-start.15
  387.2 10.9 %copy-start.8 = (f32[1,512,1024]{1,2,0:T(8,128)S(1)}, f32[1,512,1024]{1,2,0:T(8,128)}, u32[]{:S(2)}) copy-start(f32[1,512,1024]{1,2,0:T(8,128)} %copy-done.7) | copy-start | bytes 6291460 | tf_op jit(solution)/shard_map/while
  412.1 6.7 copy-start.16
  412.1 6.7 copy-start.49
  431.6 8.0 %copy-start.32 = (f32[1024,1,128]{0,2,1:T(8,128)}, f32[1024,1,128]{0,2,1:T(8,128)S(1)}, u32[]{:S(2)}) copy-start(f32[1024,1,128]{0,2,1:T(8,128)S(1)} %get-tuple-element.300) | copy-start | bytes 1572868
  431.6 8.0 %copy-start.34 = (f32[1024,1,128]{0,2,1:T(8,128)}, f32[1024,1,128]{0,2,1:T(8,128)S(1)}, u32[]{:S(2)}) copy-start(f32[1024,1,128]{0,2,1:T(8,128)S(1)} %get-tuple-element.301) | copy-start | bytes 1572868
  441.8 313.5 %all-reduce.23.cloned.1.call-start = ((), (), s32[]{:S(2)}) async-start(), calls=%async_computation.3 | async-start | bytes 13107200 | tf_op jit(solution)/shard_map/psum | solution.py:220
  443.3 8.8 %copy-start.12 = (f32[1024,640]{1,0:T(8,128)S(1)}, f32[1024,640]{1,0:T(8,128)}, u32[]{:S(2)}) copy-start(f32[1024,640]{1,0:T(8,128)} %copy-done.9) | copy-start | bytes 7864324
  443.3 8.8 %copy-start.38 = (f32[1024,512]{1,0:T(8,128)S(1)}, f32[1024,512]{1,0:T(8,128)}, u32[]{:S(2)}) copy-start(f32[1024,512]{1,0:T(8,128)} %copy-done.36) | copy-start | bytes 6291460
  443.3 8.8 %copy-start.40 = (f32[1024,512]{1,0:T(8,128)S(1)}, f32[1024,512]{1,0:T(8,128)}, u32[]{:S(2)}) copy-start(f32[1024,512]{1,0:T(8,128)} %copy-done.39) | copy-start | bytes 6291460
  452.1 7.3 copy-start.6
  452.1 7.3 copy-start.33
  452.1 7.3 copy-start.35
  452.1 12.9 %copy-start.31 = (f32[32,8,2,512]{3,1,2,0:T(8,128)S(1)}, f32[32,8,2,512]{3,1,2,0:T(8,128)}, u32[]{:S(2)}) copy-start(f32[32,8,2,512]{3,1,2,0:T(8,128)} %copy-done.29) | copy-start | bytes 3145732
  (50 other events, 186.7 us)
Sparse Core Ops, SparseCore 0:
  71.8 62.5 all-reduce.16
  159.0 59.9 all-reduce.18
  246.6 59.9 all-reduce.20
  441.9 81.6 all-reduce.24
  530.1 225.1 all-reduce.22
